TPU v7x, 32 devices: a whole 2x2x4 slice. The times are simulated.
32 devices in a mesh: col: 16 (over z, y, x), row: 2 (over core).
Axes of the slice: x: 2, y: 2, z: 4, core: 2. Of those that a mesh axis runs over, the one named last changes fastest.
Arguments:
- k_blocks: bfloat16 [2, 16, 4, 256, 256], P('row', 'col'), may hold values from -0.1875 to 0.1875
- slot_row: int32 [2, 16, 4], P('row', 'col'), may hold values from 0 to 3
- slot_col: int32 [2, 16, 4], P('row', 'col'), may hold values from 0 to 3
- live_count: int32 [2, 16], P('row', 'col'), may hold values from 1 to 4, as said below
- cost: float32 [16384], P('col'), may hold values from -6 to 6
- upper: float32 [16384], P('col'), may hold values from 0.5 to 2
- tau: float32 [16384], P('col'), may hold values from 0.2 to 0.8
- sigma: float32 [2, 1024], P('row', 'col'), may hold values from 0.2 to 0.8
- demand: float32 [2, 1024, 128], P('row', 'col'), may hold values from -6 to 6
- primal_start: float32 [16384, 128], P('col'), may hold values from 0 to 1
- dual_start: float32 [2, 1024, 128], P('row', 'col'), may hold values from 0 to 1
Outputs:
- primal: float32 [16384, 128], P('col')
- dual: float32 [2, 1024, 128], P('row', 'col')
Inputs may be any that keep to these rules, and one draw needn't show every extreme that they name: `live_count`: only slots below a device's count belong to K; the blocks in later slots are ignored. Some device has all 4 slots in use.
All inputs are finite; a program needn't handle non-finite values.
Results may differ from a plain program's by a relative error of at most 0.0023.
Values may be sent and summed in bfloat16 or wider, within the bound.
A program may use at most 64 MiB of HBM per device.

v0:
```python
import jax
import jax.numpy as jnp
from jax import lax
from jax.sharding import PartitionSpec as P

ITERS = 2


def transpose_terms(blocks, row_hot, col_hot, everyone):
    chosen = jnp.einsum(
        "kg,gis->kis", row_hot.astype(jnp.bfloat16), everyone, preferred_element_type=jnp.float32
    ).astype(jnp.bfloat16)
    terms = jnp.einsum("kij,kis->kjs", blocks, chosen, preferred_element_type=jnp.float32)
    return jnp.einsum(
        "kc,kjs->cjs", col_hot.astype(jnp.float32), terms, precision=lax.Precision.HIGHEST
    )


def forward_terms(blocks, row_hot, col_hot, extrapolated):
    chosen = jnp.einsum(
        "kc,cjs->kjs",
        col_hot.astype(jnp.bfloat16),
        extrapolated,
        preferred_element_type=jnp.float32,
    ).astype(jnp.bfloat16)
    terms = jnp.einsum("kij,kjs->kis", blocks, chosen, preferred_element_type=jnp.float32)
    return jnp.einsum(
        "kg,kis->gis", row_hot.astype(jnp.float32), terms, precision=lax.Precision.HIGHEST
    )


def on_device(
    k_blocks,
    slot_row,
    slot_col,
    live_count,
    cost,
    upper,
    tau,
    sigma,
    demand,
    primal_start,
    dual_start,
):
    blocks = k_blocks[0, 0]
    rows_of = slot_row[0, 0]
    cols_of = slot_col[0, 0]
    count = live_count[0, 0]
    slots = blocks.shape[0]
    width = blocks.shape[1]
    col_count = lax.axis_size("col")
    groups = col_count // 4
    scenarios = primal_start.shape[1]
    col_blocks = primal_start.shape[0] // width
    live = jnp.arange(slots) < count
    row_hot = (rows_of[:, None] == jnp.arange(groups)[None, :]) & live[:, None]
    col_hot = (cols_of[:, None] == jnp.arange(col_blocks)[None, :]) & live[:, None]
    primal = primal_start
    dual = dual_start[0]
    rates = sigma[0][:, None]
    needed = demand[0]
    for step in range(ITERS):
        everyone = lax.all_gather(dual.astype(jnp.bfloat16), "col", axis=0, tiled=True).reshape(
            groups, width, scenarios
        )
        per_col = transpose_terms(blocks, row_hot, col_hot, everyone)
        flat = per_col.reshape(col_blocks * width, scenarios)
        back = lax.psum(flat, "row")
        new_primal = jnp.minimum(
            jnp.maximum(primal - tau[:, None] * (cost[:, None] - back), 0.0), upper[:, None]
        )
        extrapolated = (
            (2.0 * new_primal - primal).astype(jnp.bfloat16).reshape(col_blocks, width, scenarios)
        )
        per_row = forward_terms(blocks, row_hot, col_hot, extrapolated)
        outgoing = per_row.reshape(col_count, -1, scenarios)
        incoming = lax.all_to_all(outgoing, "col", split_axis=0, concat_axis=0, tiled=True)
        forward = jnp.sum(incoming, axis=0)
        dual = jnp.maximum(dual + rates * (needed - forward), 0.0)
        primal = new_primal
    return (primal, dual[None])


def solution(mesh):
    in_specs = (
        P("row", "col", None, None, None),
        P("row", "col", None),
        P("row", "col", None),
        P("row", "col"),
        P("col"),
        P("col"),
        P("col"),
        P("row", "col"),
        P("row", "col", None),
        P("col", None),
        P("row", "col", None),
    )
    out_specs = (P("col", None), P("row", "col", None))
    return jax.shard_map(
        on_device, mesh=mesh, in_specs=in_specs, out_specs=out_specs, check_vma=False
    )
```

profile of v0, /device:TPU:0, one launch (start us, length us, event | category | flops | bytes accessed | tf_op | source)
XLA Modules:
  0.0 186.3 jit_solution(3237687826428789127)
XLA Ops:
  7.9 0.8 bitcast_convert_fusion
  8.7 43.8 %all_gather.6 = bf16[1024,128]{1,0:T(8,128)(2,1)S(1)} all-gather(bf16[64,128]{1,0:T(8,128)(2,1)S(1)} %bitcast_convert_fusion), channel_id=1, replica_groups=mesh['col'=16,'row'=2] {'col'}, dimensions={0}, use_global_device_ids=true | all-gather | bytes 278528 | tf_op jit(solution)/shard_map/all_gather | solution.py:63
  52.5 0.7 copy-done.9
  53.1 0.4 fusion.22
  53.5 0.3 fusion.14
  53.8 0.2 copy.19
  54.0 0.6 fusion.6
  54.6 0.8 copy.13
  55.5 0.0 all-reduce.5.cloned.1.call-start
  55.6 14.7 %all-reduce.3.cloned.1.call-done = f32[1024,128]{1,0:T(8,128)} async-done(((f32[1024,128]{1,0:T(8,128)}), f32[1024,128]{1,0:T(8,128)}) %all-reduce.3.cloned.1.call-update) | async-done | bytes 524304 | tf_op jit(solution)/shard_map/psum | solution.py:68
  70.3 1.5 subtract_convert_fusion.1
  71.8 0.4 fusion.20
  72.2 0.3 fusion.12
  72.5 0.2 copy.22
  72.7 0.6 fusion.4
  73.4 22.1 %all_to_all.10 = f32[16,64,128]{2,1,0:T(8,128)S(1)} all-to-all(f32[16,64,128]{2,1,0:T(8,128)S(1)} %bitcast.79), channel_id=1, replica_groups=mesh['col'=16,'row'=2] {'col'}, dimensions={0} | all-to-all | bytes 1048576 | tf_op jit(solution)/shard_map/all_to_all | solution.py:77
  95.5 0.7 copy-done.3
  96.2 0.1 fusion.33
  96.3 39.5 %all_gather.7 = bf16[1024,128]{1,0:T(8,128)(2,1)S(1)} all-gather(bf16[64,128]{1,0:T(8,128)(2,1)S(1)} %fusion.33), channel_id=1, replica_groups=mesh['col'=16,'row'=2] {'col'}, dimensions={0}, use_global_device_ids=true | all-gather | bytes 278528 | tf_op jit(solution)/shard_map/all_gather | solution.py:63
  135.7 0.4 fusion.18
  136.1 0.3 fusion.10
  136.4 0.2 copy.25
  136.6 0.6 fusion.2
  137.2 0.8 copy.15
  138.1 14.8 %all-reduce.5.cloned.1.call-done = f32[1024,128]{1,0:T(8,128)} async-done(((f32[1024,128]{1,0:T(8,128)}), f32[1024,128]{1,0:T(8,128)}) %all-reduce.5.cloned.1.call-update) | async-done | bytes 524304 | tf_op jit(solution)/shard_map/psum | solution.py:68
  152.8 2.3 %subtract_convert_fusion = (bf16[1024,128]{1,0:T(8,128)(2,1)S(1)}, f32[1024,128]{1,0:T(8,128)}) fusion(f32[1024]{0:T(1024)S(1)} %copy-done.5, f32[1024,128]{1,0:T(8,128)S(1)} %copy-done.1, f32[1024,128]{1,0:T(8,128)S(1)} %copy-done.2, f32[1024]{0:T(1024)S(1)} %copy-done.6, f32[1024]{0:T(1024)S(1)} %copy-done.7, f32[1024,128]{1,0:T(8,128)} %all-reduce.5.cloned.1.call-done), kind=kLoop, calls=%fused_computation.20 | loop fusion | flops 1703936 | bytes 2371584 | tf_op jit(solution)/shard_map/convert_element_type | solution.py:73
  155.1 0.4 fusion.16
  155.5 0.3 fusion.8
  155.8 0.2 copy.28
  156.1 0.6 fusion
  156.7 22.1 %all_to_all.11 = f32[16,64,128]{2,1,0:T(8,128)S(1)} all-to-all(f32[16,64,128]{2,1,0:T(8,128)S(1)} %bitcast.80), channel_id=1, replica_groups=mesh['col'=16,'row'=2] {'col'}, dimensions={0} | all-to-all | bytes 1048576 | tf_op jit(solution)/shard_map/all_to_all | solution.py:77
  178.8 0.7 fusion.26
  (29 shorter events, 0.3 us)
Async XLA Ops:
  7.2 46.3 %copy-start = (bf16[1,1,4,256,256]{4,3,2,1,0:T(8,128)(2,1)S(1)}, bf16[1,1,4,256,256]{4,3,2,1,0:T(8,128)(2,1)}, u32[]{:S(2)}) copy-start(bf16[1,1,4,256,256]{4,3,2,1,0:T(8,128)(2,1)} %param.11) | copy-start | bytes 1572868
  7.2 63.1 %all-reduce.3.cloned.1.call-start = ((), (), s32[]{:S(2)}) async-start(), calls=%async_computation.2 | async-start | bytes 1048576 | tf_op jit(solution)/shard_map/psum | solution.py:68
  52.5 0.7 copy-start.9
  52.5 0.7 copy-start.10
  54.6 15.6 %copy-start.6 = (f32[1024]{0:T(1024)S(1)}, f32[1024]{0:T(1024)}, u32[]{:S(2)}) copy-start(f32[1024]{0:T(1024)} %param.15) | copy-start | bytes 12292
  54.6 15.6 %copy-start.7 = (f32[1024]{0:T(1024)S(1)}, f32[1024]{0:T(1024)}, u32[]{:S(2)}) copy-start(f32[1024]{0:T(1024)} %param.17) | copy-start | bytes 12292
  55.5 14.8 %copy-start.1 = (f32[1024,128]{1,0:T(8,128)S(1)}, f32[1024,128]{1,0:T(8,128)}, u32[]{:S(2)}) copy-start(f32[1024,128]{1,0:T(8,128)} %param.20) | copy-start | bytes 1572868
  55.5 14.8 %copy-start.5 = (f32[1024]{0:T(1024)S(1)}, f32[1024]{0:T(1024)}, u32[]{:S(2)}) copy-start(f32[1024]{0:T(1024)} %param.16) | copy-start | bytes 12292
  55.5 97.3 %all-reduce.5.cloned.1.call-start = ((), (), s32[]{:S(2)}) async-start(), calls=%async_computation.3 | async-start | bytes 1048576 | tf_op jit(solution)/shard_map/psum | solution.py:68
  95.4 0.8 copy-start.3
  95.4 0.8 copy-start.4
  95.5 0.7 copy-start.8
  138.0 14.8 %copy-start.2 = (f32[1024,128]{1,0:T(8,128)S(1)}, f32[1024,128]{1,0:T(8,128)}, u32[]{:S(2)}) copy-start(f32[1024,128]{1,0:T(8,128)} %all-reduce.3.cloned.1.call-done) | copy-start | bytes 1572868
Sparse Core Ops, SparseCore 0:
  55.6 14.5 all-reduce.2
  138.2 14.5 all-reduce.4
where the time goes:
time: 187 us; the launch traced here: 186 us
  blocking collectives  127 us (68%)
  waiting for transfers between devices  29.5 us (16%)
  between operations  14.9 us (8%)
  other arithmetic  5.45 us (3%)
  matrix products  4.98 us (3%)
  local copies, waits for them, and re-layouts  4.08 us (2%)
    all_gather x2, blocking collectives, on_device(): lax.all_gather(dual.astype(jnp.bfloat16), 'col', axis=0, tiled=True)  83.2 us
    all_to_all x2, blocking collectives, on_device(): lax.all_to_all(outgoing, 'col', split_axis=0, concat_axis=0, tiled=True)  44.1 us
    psum x2, waiting for transfers between devices, on_device(): back = lax.psum(flat, 'row')  29.5 us
    convert_element_type x2, other arithmetic, on_device(): (2.0 * new_primal - primal).astype(jnp.bfloat16)  3.83 us
  transfers between devices with their start and end apart: 2, of which 2 were waited for; matrix products, arithmetic and copies ran while one was open for 0% of the time, Pallas kernels for 0%

commit v1 on v0

v1 whole, which is shorter than its diff:
```python
import functools

import jax
import jax.numpy as jnp
from jax import lax
from jax.experimental import pallas as pl
from jax.experimental.pallas import tpu as pltpu
from jax.sharding import PartitionSpec as P

ITERS = 2
MESH = pl.DeviceIdType.MESH
F32 = jnp.float32
BF16 = jnp.bfloat16


def spread(vector, lanes):
    n = vector.shape[1]
    at_row = lax.broadcasted_iota(jnp.int32, (n, n), 0)
    at_col = lax.broadcasted_iota(jnp.int32, (n, n), 1)
    picked = jnp.where(at_row == at_col, jnp.broadcast_to(vector, (n, n)), 0.0)
    return jnp.broadcast_to(jnp.sum(picked, axis=1, keepdims=True), (n, lanes))


def kernel(
    sizes,
    slot_row,
    slot_col,
    live_count,
    k_hbm,
    cost_ref,
    upper_ref,
    tau_ref,
    sigma_ref,
    demand_hbm,
    primal_hbm,
    dual_hbm,
    primal_out,
    dual_out,
    blocks,
    blocks_t,
    primal,
    dual,
    demand,
    cost,
    upper,
    tau,
    sigma,
    terms,
    extrapolated,
    everyones,
    pairs,
    outgoings,
    plane_ins,
    column_outs,
    column_ins,
    local_sem,
    gather_send,
    gather_recv,
    pair_send,
    pair_recv,
    plane_send,
    plane_recv,
    column_send,
    column_recv,
):
    zs, ps, rs = sizes
    slots, width, _ = blocks.shape
    own = width // ps
    col_blocks = extrapolated.shape[0]
    scenarios = dual.shape[1]
    col = lax.axis_index("col")
    row = lax.axis_index("row")
    z, p = col // ps, lax.rem(col, ps)

    def z_peer(d):
        return {"col": lax.rem(z + d, zs) * ps + p}

    def p_peer(e):
        return {"col": z * ps + lax.rem(p + e, ps)}

    def r_peer(f):
        return {"row": lax.rem(row + f, rs)}

    def back_z(d):
        return lax.rem(z - d + zs, zs)

    mine = pl.ds(pl.multiple_of(p * own, own), own)

    loads = [
        pltpu.make_async_copy(src, dst, local_sem.at[i])
        for i, (src, dst) in enumerate(
            (
                (dual_hbm.at[0], dual),
                (k_hbm.at[0, 0], blocks),
                (primal_hbm, primal),
                (demand_hbm.at[0], demand),
            )
        )
    ]
    for load in loads:
        load.start()

    barrier = pltpu.get_barrier_semaphore()
    peers = (
        [z_peer(d) for d in range(1, zs)]
        + [p_peer(e) for e in range(1, ps)]
        + [r_peer(f) for f in range(1, rs)]
    )
    for peer in peers:
        pl.semaphore_signal(barrier, inc=1, device_id=peer, device_id_type=MESH)

    live = live_count[0, 0]
    alive = [k < live for k in range(slots)]
    rows_of = [slot_row[0, 0, k] for k in range(slots)]
    cols_of = [slot_col[0, 0, k] for k in range(slots)]

    loads[0].wait()
    everyones[0][z, mine, :] = dual[...].astype(BF16)

    chunk = cost_ref.shape[1]
    for i in range(cost_ref.shape[0]):
        at = pl.ds(i * chunk, chunk)
        cost[at, :] = spread(cost_ref[i : i + 1, :], scenarios)
        upper[at, :] = spread(upper_ref[i : i + 1, :], scenarios)
        tau[at, :] = spread(tau_ref[i : i + 1, :], scenarios)
    sigma[...] = spread(sigma_ref[...], scenarios)
    loads[1].wait()
    for k in range(slots):
        blocks_t[k] = blocks[k].T

    pl.semaphore_wait(barrier, len(peers))

    sent = []
    waited = [loads[2], loads[3]]
    stores = []

    def remote(src, dst, send_sem, recv_sem, peer):
        copy = pltpu.make_async_remote_copy(
            src_ref=src,
            dst_ref=dst,
            send_sem=send_sem,
            recv_sem=recv_sem,
            device_id=peer,
            device_id_type=MESH,
        )
        copy.start()
        sent.append(copy)
        return copy

    for it in range(ITERS):
        everyone, pair, outgoing = everyones[it], pairs[it], outgoings[it]
        plane_in, column_out, column_in = plane_ins[it], column_outs[it], column_ins[it]

        def pass_on(d, e):
            part = everyone.at[back_z(d), mine, :]
            return remote(
                part, part, gather_send.at[it, d, e], gather_recv.at[it, d, e], p_peer(e)
            )

        own_part = everyone.at[z, mine, :]
        along_z = [
            remote(
                own_part, own_part, gather_send.at[it, d, 0], gather_recv.at[it, d, 0], z_peer(d)
            )
            for d in range(1, zs)
        ]
        in_plane = [pass_on(0, e) for e in range(1, ps)]
        for d in range(1, zs):
            along_z[d - 1].wait_recv()
            in_plane += [pass_on(d, e) for e in range(1, ps)]
        for copy in in_plane:
            copy.wait_recv()

        for k in range(slots):
            terms[k] = jnp.dot(blocks_t[k], everyone[rows_of[k]], preferred_element_type=F32)
        exchanged = []
        for c in range(col_blocks):
            total = jnp.zeros((width, scenarios), F32)
            for k in range(slots):
                hit = jnp.logical_and(alive[k], cols_of[k] == c)
                total = total + jnp.where(hit, terms[k], 0.0)
            pair[row, c] = total.astype(BF16)
            part = pair.at[row, c]
            exchanged.append(
                [
                    remote(part, part, pair_send.at[it, f, c], pair_recv.at[it, f, c], r_peer(f))
                    for f in range(1, rs)
                ]
            )
        for load in waited:
            load.wait()
        waited = []
        for c in range(col_blocks):
            for copy in exchanged[c]:
                copy.wait_recv()
            at = pl.ds(c * width, width)
            back = pair[0, c].astype(F32)
            for r in range(1, rs):
                back = back + pair[r, c].astype(F32)
            old = primal[at, :]
            new = jnp.minimum(
                jnp.maximum(old - tau[at, :] * (cost[at, :] - back), 0.0), upper[at, :]
            )
            extrapolated[c] = (2.0 * new - old).astype(BF16)
            primal[at, :] = new
        if it == ITERS - 1:
            store = pltpu.make_async_copy(primal, primal_out, local_sem.at[0])
            store.start()
            stores.append(store)

        for k in range(slots):
            terms[k] = jnp.dot(blocks[k], extrapolated[cols_of[k]], preferred_element_type=F32)
        for g in range(zs):
            total = jnp.zeros((width, scenarios), F32)
            for k in range(slots):
                hit = jnp.logical_and(alive[k], rows_of[k] == g)
                total = total + jnp.where(hit, terms[k], 0.0)
            outgoing[g] = total.astype(BF16)
        planes = []
        for e in range(1, ps):
            theirs = pl.ds(pl.multiple_of(lax.rem(p + e, ps) * own, own), own)
            planes.append(
                remote(
                    outgoing.at[:, theirs, :],
                    plane_in.at[e - 1],
                    plane_send.at[it, e],
                    plane_recv.at[it, e],
                    p_peer(e),
                )
            )
        for copy in planes:
            copy.wait_recv()

        def plane_sum(g):
            total = outgoing[g, mine, :].astype(F32)
            for e in range(1, ps):
                total = total + plane_in[e - 1, g].astype(F32)
            return total

        columns = []
        for d in range(1, zs):
            column_out[d - 1] = plane_sum(lax.rem(z + d, zs)).astype(BF16)
            columns.append(
                remote(
                    column_out.at[d - 1],
                    column_in.at[d - 1],
                    column_send.at[it, d],
                    column_recv.at[it, d],
                    z_peer(d),
                )
            )
        forward = plane_sum(z)
        for d in range(1, zs):
            columns[d - 1].wait_recv()
            forward = forward + column_in[d - 1].astype(F32)
        new_dual = jnp.maximum(dual[...] + sigma[...] * (demand[...] - forward), 0.0)
        dual[...] = new_dual
        if it < ITERS - 1:
            everyones[it + 1][z, mine, :] = new_dual.astype(BF16)

    store = pltpu.make_async_copy(dual, dual_out.at[0], local_sem.at[1])
    store.start()
    stores.append(store)
    for copy in sent:
        copy.wait_send()
    for store in stores:
        store.wait()


def on_device(
    k_blocks,
    slot_row,
    slot_col,
    live_count,
    cost,
    upper,
    tau,
    sigma,
    demand,
    primal_start,
    dual_start,
):
    _, _, slots, width, _ = k_blocks.shape
    _, own, scenarios = dual_start.shape
    variables = primal_start.shape[0]
    col_blocks = variables // width
    rs = lax.axis_size("row")
    ps = width // own
    zs = lax.axis_size("col") // ps
    flat = lambda v: v.reshape(-1, 128)
    smem = pl.BlockSpec(memory_space=pltpu.SMEM)
    vmem = pl.BlockSpec(memory_space=pltpu.VMEM)
    anywhere = pl.BlockSpec(memory_space=pl.ANY)
    dma = pltpu.SemaphoreType.DMA
    twice = lambda shape, kind: [pltpu.VMEM(shape, kind) for _ in range(ITERS)]
    return pl.pallas_call(
        functools.partial(kernel, (zs, ps, rs)),
        out_shape=(
            jax.ShapeDtypeStruct(primal_start.shape, F32),
            jax.ShapeDtypeStruct(dual_start.shape, F32),
        ),
        in_specs=[smem] * 3 + [anywhere] + [vmem] * 4 + [anywhere] * 3,
        out_specs=(anywhere, anywhere),
        scratch_shapes=[
            pltpu.VMEM((slots, width, width), BF16),
            pltpu.VMEM((slots, width, width), BF16),
            pltpu.VMEM((variables, scenarios), F32),
            pltpu.VMEM((own, scenarios), F32),
            pltpu.VMEM((own, scenarios), F32),
            pltpu.VMEM((variables, scenarios), F32),
            pltpu.VMEM((variables, scenarios), F32),
            pltpu.VMEM((variables, scenarios), F32),
            pltpu.VMEM((own, scenarios), F32),
            pltpu.VMEM((slots, width, scenarios), F32),
            pltpu.VMEM((col_blocks, width, scenarios), BF16),
            twice((zs, width, scenarios), BF16),
            twice((rs, col_blocks, width, scenarios), BF16),
            twice((zs, width, scenarios), BF16),
            twice((ps - 1, zs, own, scenarios), BF16),
            twice((zs - 1, own, scenarios), BF16),
            twice((zs - 1, own, scenarios), BF16),
            dma((4,)),
            dma((ITERS, zs, ps)),
            dma((ITERS, zs, ps)),
            dma((ITERS, rs, col_blocks)),
            dma((ITERS, rs, col_blocks)),
            dma((ITERS, ps)),
            dma((ITERS, ps)),
            dma((ITERS, zs)),
            dma((ITERS, zs)),
        ],
        compiler_params=pltpu.CompilerParams(
            collective_id=0, has_side_effects=True, vmem_limit_bytes=40 * 1024 * 1024
        ),
        cost_estimate=pl.CostEstimate(
            flops=ITERS * 4 * slots * width * width * scenarios,
            bytes_accessed=2 * slots * width * width + 8 * variables * scenarios,
            transcendentals=0,
        ),
    )(
        slot_row,
        slot_col,
        live_count,
        k_blocks,
        flat(cost),
        flat(upper),
        flat(tau),
        sigma,
        demand,
        primal_start,
        dual_start,
    )


def solution(mesh):
    in_specs = (
        P("row", "col", None, None, None),
        P("row", "col", None),
        P("row", "col", None),
        P("row", "col"),
        P("col"),
        P("col"),
        P("col"),
        P("row", "col"),
        P("row", "col", None),
        P("col", None),
        P("row", "col", None),
    )
    out_specs = (P("col", None), P("row", "col", None))
    return jax.shard_map(
        on_device, mesh=mesh, in_specs=in_specs, out_specs=out_specs, check_vma=False
    )
```

time: 187 us -> 50.5 us (0.27)
  blocking collectives: 127 us -> 0 us
  Pallas kernels: 0 us -> 41.7 us
  waiting for transfers between devices: 29.5 us -> 0 us
  between operations: 14.9 us -> 1.35 us
  other arithmetic: 5.45 us -> 0 us
  matrix products: 4.98 us -> 0 us
  local copies, waits for them, and re-layouts: 4.08 us -> 7.04 us
    all_gather x2 -> x0, blocking collectives: 83.2 us -> none  [on_device(): lax.all_gather(dual.astype(jnp.bfloat16), 'col', axis=0, tiled=True)]
    all_to_all x2 -> x0, blocking collectives: 44.1 us -> none  [on_device(): lax.all_to_all(outgoing, 'col', split_axis=0, concat_axis=0, tiled=True)]
    pallas_call x0 -> x1, Pallas kernels: none -> 41.7 us  [on_device(): pl.pallas_call(functools.partial(kernel, (zs, ps, rs)), out_shape=(jax.Sh...]
    psum x2 -> x0, waiting for transfers between devices: 29.5 us -> none  [on_device(): back = lax.psum(flat, 'row')]
    unnamed x22, local copies, waits for them, and re-layouts: 1.44 us -> 7.04 us
    dot_general x12 -> x0, matrix products: 4.98 us -> none  [the longest x2 1.19 us: transpose_terms(): jnp.einsum('kc,kjs->cjs', col_hot.astype(jnp.float32), terms, precision=l...]
    convert_element_type x4 -> x0, other arithmetic: 4.67 us -> none  [the longest x2 3.83 us: on_device(): (2.0 * new_primal - primal).astype(jnp.bfloat16)]
    dot_general x8 -> x0, local copies, waits for them, and re-layouts: 2.65 us -> none  [the longest x2 1.66 us: transpose_terms(): jnp.einsum('kc,kjs->cjs', col_hot.astype(jnp.float32), terms, precision=l...]
  transfers between devices with their start and end apart: 2 -> 0, of which waited for: 2 -> 0; matrix products, arithmetic and copies ran while one was open for 0% -> 0% of each run, Pallas kernels for 0% -> 0%
where the time goes in v1:
time: 50.5 us; the launch traced here: 50.1 us
  Pallas kernels  41.7 us (83%)
  local copies, waits for them, and re-layouts  7.04 us (14%)
  between operations  1.35 us (3%)
    pallas_call x1, Pallas kernels, on_device(): pl.pallas_call(functools.partial(kernel, (zs, ps, rs)), out_shape=(jax.Sh...  41.7 us
    unnamed x22, local copies, waits for them, and re-layouts  7.04 us

profile of v1, /device:TPU:0, one launch (start us, length us, event | category | flops | bytes accessed | tf_op | source)
XLA Modules:
  0.0 50.1 jit_solution(14814590630370819602)
XLA Ops:
  0.6 0.0 copy-start.4
  1.3 0.0 copy-start.7
  1.3 0.0 copy-start.8
  1.3 0.0 copy-start.9
  1.3 0.0 copy-done.4
  1.3 0.6 %copy-done.7 = s32[1,1,4]{2,1,0:T(1,128)S(1)} copy-done((s32[1,1,4]{2,1,0:T(1,128)S(1)}, s32[1,1,4]{2,1,0:T(1,128)}, u32[]{:S(2)}) %copy-start.7) | copy-done | bytes 40
  2.0 0.0 copy-done.8
  2.0 0.0 copy-done.9
  2.0 0.0 copy-start
  2.0 1.0 %copy-done = bf16[1,1,4,256,256]{4,3,2,1,0:T(8,128)(2,1)S(1)} copy-done((bf16[1,1,4,256,256]{4,3,2,1,0:T(8,128)(2,1)S(1)}, bf16[1,1,4,256,256]{4,3,2,1,0:T(8,128)(2,1)}, u32[]{:S(2)}) %copy-start) | copy-done | bytes 524312
  3.0 0.0 copy-start.1
  3.0 1.0 %copy-done.1 = f32[1024,128]{1,0:T(8,128)S(1)} copy-done((f32[1024,128]{1,0:T(8,128)S(1)}, f32[1024,128]{1,0:T(8,128)}, u32[]{:S(2)}) %copy-start.1) | copy-done | bytes 524312
  4.1 0.0 copy-start.2
  4.1 0.8 %copy-done.2 = f32[1,64,128]{2,1,0:T(8,128)S(1)} copy-done((f32[1,64,128]{2,1,0:T(8,128)S(1)}, f32[1,64,128]{2,1,0:T(8,128)}, u32[]{:S(2)}) %copy-start.2) | copy-done | bytes 32792
  4.8 0.0 copy-start.3
  4.8 0.8 %copy-done.3 = f32[1,64,128]{2,1,0:T(8,128)S(1)} copy-done((f32[1,64,128]{2,1,0:T(8,128)S(1)}, f32[1,64,128]{2,1,0:T(8,128)}, u32[]{:S(2)}) %copy-start.3) | copy-done | bytes 32792
  5.6 0.0 copy-start.5
  5.6 0.7 %copy-done.5 = f32[1024]{0:T(1024)S(1)} copy-done((f32[1024]{0:T(1024)S(1)}, f32[1024]{0:T(1024)}, u32[]{:S(2)}) %copy-start.5) | copy-done | bytes 4120
  6.3 0.0 copy-start.6
  6.3 0.7 %copy-done.6 = f32[1024]{0:T(1024)S(1)} copy-done((f32[1024]{0:T(1024)S(1)}, f32[1024]{0:T(1024)}, u32[]{:S(2)}) %copy-start.6) | copy-done | bytes 4120
  7.0 41.7 %shard_map.122 = (f32[1024,128]{1,0:T(8,128)S(1)}, f32[1,64,128]{2,1,0:T(8,128)S(1)}) custom-call(s32[1,1,4]{2,1,0:T(1,128)S(1)} %copy-done.7, s32[1,1,4]{2,1,0:T(1,128)S(1)} %copy-done.8, s32[1,1]{1,0:T(1,128)S(6)} %copy.15.live_count, bf16[1,1,4,256,256]{4,3,2,1,0:T(8,128)(2,1)S(1)} %copy-done, f32[8,128]{1,0:T(8,128)S(1)} %bitcast.3, ...), custom_call_target="tpu_custom_call" | custom-call | flops 268435456 | bytes 1572864 | tf_op jit(solution)/shard_map/pallas_call | solution.py:296
  48.7 0.8 %copy.16 = f32[1024,128]{1,0:T(8,128)} copy(f32[1024,128]{1,0:T(8,128)S(1)} %get-tuple-element.4) | data formatting | bytes 1048576
  49.5 0.6 %copy.17 = f32[1,64,128]{2,1,0:T(8,128)} copy(f32[1,64,128]{2,1,0:T(8,128)S(1)} %get-tuple-element.5) | data formatting | bytes 65536
Async XLA Ops:
  0.6 0.7 %copy-start.4 = (f32[1024]{0:T(1024)S(1)}, f32[1024]{0:T(1024)}, u32[]{:S(2)}) copy-start(f32[1024]{0:T(1024)} %param.15) | copy-start | bytes 12292
  1.3 0.7 %copy-start.7 = (s32[1,1,4]{2,1,0:T(1,128)S(1)}, s32[1,1,4]{2,1,0:T(1,128)}, u32[]{:S(2)}) copy-start(s32[1,1,4]{2,1,0:T(1,128)} %slot_row.1) | copy-start | bytes 52
  1.3 0.7 %copy-start.8 = (s32[1,1,4]{2,1,0:T(1,128)S(1)}, s32[1,1,4]{2,1,0:T(1,128)}, u32[]{:S(2)}) copy-start(s32[1,1,4]{2,1,0:T(1,128)} %slot_col.1) | copy-start | bytes 52
  1.3 0.7 %copy-start.9 = (f32[1,64]{1,0:T(1,128)S(1)}, f32[1,64]{1,0:T(1,128)}, u32[]{:S(2)}) copy-start(f32[1,64]{1,0:T(1,128)} %sigma_ref.1) | copy-start | bytes 772
  2.0 1.0 %copy-start = (bf16[1,1,4,256,256]{4,3,2,1,0:T(8,128)(2,1)S(1)}, bf16[1,1,4,256,256]{4,3,2,1,0:T(8,128)(2,1)}, u32[]{:S(2)}) copy-start(bf16[1,1,4,256,256]{4,3,2,1,0:T(8,128)(2,1)} %k_hbm.1) | copy-start | bytes 1572868
  3.0 1.0 %copy-start.1 = (f32[1024,128]{1,0:T(8,128)S(1)}, f32[1024,128]{1,0:T(8,128)}, u32[]{:S(2)}) copy-start(f32[1024,128]{1,0:T(8,128)} %primal_hbm.1) | copy-start | bytes 1572868
  4.1 0.8 %copy-start.2 = (f32[1,64,128]{2,1,0:T(8,128)S(1)}, f32[1,64,128]{2,1,0:T(8,128)}, u32[]{:S(2)}) copy-start(f32[1,64,128]{2,1,0:T(8,128)} %demand_hbm.1) | copy-start | bytes 98308
  4.8 0.8 %copy-start.3 = (f32[1,64,128]{2,1,0:T(8,128)S(1)}, f32[1,64,128]{2,1,0:T(8,128)}, u32[]{:S(2)}) copy-start(f32[1,64,128]{2,1,0:T(8,128)} %dual_hbm.1) | copy-start | bytes 98308
  5.6 0.7 %copy-start.5 = (f32[1024]{0:T(1024)S(1)}, f32[1024]{0:T(1024)}, u32[]{:S(2)}) copy-start(f32[1024]{0:T(1024)} %param.16) | copy-start | bytes 12292
  6.3 0.7 %copy-start.6 = (f32[1024]{0:T(1024)S(1)}, f32[1024]{0:T(1024)}, u32[]{:S(2)}) copy-start(f32[1024]{0:T(1024)} %param.17) | copy-start | bytes 12292

commit v2 on v1

v2 whole, which is shorter than its diff:
```python
import functools

import jax
import jax.numpy as jnp
from jax import lax
from jax.experimental import pallas as pl
from jax.experimental.pallas import tpu as pltpu
from jax.sharding import PartitionSpec as P

ITERS = 2
MESH = pl.DeviceIdType.MESH
F32 = jnp.float32
BF16 = jnp.bfloat16


def spread(vector, lanes):
    n = vector.shape[1]
    at_row = lax.broadcasted_iota(jnp.int32, (n, n), 0)
    at_col = lax.broadcasted_iota(jnp.int32, (n, n), 1)
    picked = jnp.where(at_row == at_col, jnp.broadcast_to(vector, (n, n)), 0.0)
    return jnp.broadcast_to(jnp.sum(picked, axis=1, keepdims=True), (n, lanes))


def kernel(
    sizes,
    slot_row_hbm,
    slot_col_hbm,
    live_count_hbm,
    k_hbm,
    cost_hbm,
    upper_hbm,
    tau_hbm,
    sigma_hbm,
    demand_hbm,
    primal_hbm,
    dual_hbm,
    primal_out,
    dual_out,
    slot_row,
    slot_col,
    live_count,
    cost_ref,
    upper_ref,
    tau_ref,
    sigma_ref,
    blocks,
    blocks_t,
    primal,
    dual,
    demand,
    cost,
    upper,
    tau,
    sigma,
    terms,
    extrapolated,
    everyones,
    pairs,
    outgoings,
    totals,
    column_sums,
    ahead,
    plane_ins,
    column_outs,
    column_ins,
    last_outs,
    last_ins,
    local_sem,
    gather_send,
    gather_recv,
    pair_send,
    pair_recv,
    plane_send,
    plane_recv,
    column_send,
    column_recv,
    start_send,
    start_recv,
    last_send,
    last_recv,
):
    zs, ps, rs = sizes
    slots, width, _ = blocks.shape
    own = width // ps
    col_blocks = extrapolated.shape[0]
    scenarios = dual.shape[2]
    col = lax.axis_index("col")
    row = lax.axis_index("row")
    z, p = col // ps, lax.rem(col, ps)

    def z_peer(d):
        return {"col": lax.rem(z + d, zs) * ps + p}

    def p_peer(e):
        return {"col": z * ps + lax.rem(p + e, ps)}

    def r_peer(f):
        return {"row": lax.rem(row + f, rs)}

    def back_z(d):
        return lax.rem(z - d + zs, zs)

    mine = pl.ds(pl.multiple_of(p * own, own), own)

    loads = [
        pltpu.make_async_copy(src, dst, local_sem.at[i])
        for i, (src, dst) in enumerate(
            (
                (dual_hbm.at[0], dual.at[z]),
                (k_hbm.at[0, 0], blocks),
                (primal_hbm, primal),
                (demand_hbm.at[0], demand),
                (cost_hbm, cost_ref),
                (upper_hbm, upper_ref),
                (tau_hbm, tau_ref),
                (sigma_hbm, sigma_ref.at[z]),
                (slot_row_hbm, slot_row),
                (slot_col_hbm, slot_col),
                (live_count_hbm, live_count),
            )
        )
    ]
    for load in loads:
        load.start()

    barrier = pltpu.get_barrier_semaphore()
    peers = (
        [z_peer(d) for d in range(1, zs)]
        + [p_peer(e) for e in range(1, ps)]
        + [r_peer(f) for f in range(1, rs)]
    )
    for peer in peers:
        pl.semaphore_signal(barrier, inc=1, device_id=peer, device_id_type=MESH)

    loads[0].wait()
    everyones[0][z, mine, :] = dual[z].astype(BF16)

    for load in loads[3:8]:
        load.wait()
    chunk = cost_ref.shape[1]
    for i in range(cost_ref.shape[0]):
        at = pl.ds(i * chunk, chunk)
        cost[at, :] = spread(cost_ref[i : i + 1, :], scenarios)
        upper[at, :] = spread(upper_ref[i : i + 1, :], scenarios)
        tau[at, :] = spread(tau_ref[i : i + 1, :], scenarios)
    loads[1].wait()
    ahead[z] = dual[z] + spread(sigma_ref[z], scenarios) * demand[...]
    for k in range(slots):
        blocks_t[k] = blocks[k].T
    for load in loads[8:]:
        load.wait()
    live = live_count[0, 0]
    alive = [k < live for k in range(slots)]
    rows_of = [slot_row[0, 0, k] for k in range(slots)]
    cols_of = [slot_col[0, 0, k] for k in range(slots)]

    pl.semaphore_wait(barrier, len(peers))

    sent = []
    waited = [loads[2]]
    stores = []

    def remote(src, dst, send_sem, recv_sem, peer):
        copy = pltpu.make_async_remote_copy(
            src_ref=src,
            dst_ref=dst,
            send_sem=send_sem,
            recv_sem=recv_sem,
            device_id=peer,
            device_id_type=MESH,
        )
        copy.start()
        sent.append(copy)
        return copy

    for it in range(ITERS):
        everyone, pair, outgoing = everyones[it], pairs[it], outgoings[it]
        plane_in = plane_ins[it]

        def pass_on(g, e):
            part = everyone.at[g, mine, :]
            return remote(
                part, part, gather_send.at[it, g, e], gather_recv.at[it, g, e], p_peer(e)
            )

        in_plane = []
        if it == 0:
            own_part = everyone.at[z, mine, :]
            along_z = [
                remote(own_part, own_part, start_send.at[0, d], start_recv.at[0, d], z_peer(d))
                for d in range(1, zs)
            ]
            in_plane += [pass_on(z, e) for e in range(1, ps)]
            for d in range(1, zs):
                along_z[d - 1].wait_recv()
                in_plane += [pass_on(back_z(d), e) for e in range(1, ps)]
        else:
            for g in range(zs):
                forward = column_sums[g]
                for d in range(1, zs):
                    columns[g][d - 1].wait_recv()
                    forward = forward + column_ins[g, d - 1].astype(F32)
                new_dual = jnp.maximum(ahead[g] - sigma[g] * forward, 0.0)
                dual[g] = new_dual
                everyone[g, mine, :] = new_dual.astype(BF16)
                in_plane += [pass_on(g, e) for e in range(1, ps)]
        for copy in in_plane:
            copy.wait_recv()
        if it == 0:
            fetched = [
                remote(ref.at[z], ref.at[z], start_send.at[i, d], start_recv.at[i, d], z_peer(d))
                for i, ref in ((1, sigma_ref), (2, ahead))
                for d in range(1, zs)
            ]

        for k in range(slots):
            terms[k] = jnp.dot(blocks_t[k], everyone[rows_of[k]], preferred_element_type=F32)
        exchanged = []
        for c in range(col_blocks):
            total = jnp.zeros((width, scenarios), F32)
            for k in range(slots):
                hit = jnp.logical_and(alive[k], cols_of[k] == c)
                total = total + jnp.where(hit, terms[k], 0.0)
            pair[row, c] = total
            part = pair.at[row, c]
            exchanged.append(
                [
                    remote(part, part, pair_send.at[it, f, c], pair_recv.at[it, f, c], r_peer(f))
                    for f in range(1, rs)
                ]
            )
        for load in waited:
            load.wait()
        waited = []
        for c in range(col_blocks):
            for copy in exchanged[c]:
                copy.wait_recv()
            at = pl.ds(c * width, width)
            back = pair[0, c]
            for r in range(1, rs):
                back = back + pair[r, c]
            old = primal[at, :]
            new = jnp.minimum(
                jnp.maximum(old - tau[at, :] * (cost[at, :] - back), 0.0), upper[at, :]
            )
            extrapolated[c] = (2.0 * new - old).astype(BF16)
            primal[at, :] = new
        if it == ITERS - 1:
            store = pltpu.make_async_copy(primal, primal_out, local_sem.at[0])
            store.start()
            stores.append(store)

        for k in range(slots):
            terms[k] = jnp.dot(blocks[k], extrapolated[cols_of[k]], preferred_element_type=F32)
        planes = []
        order = list(range(zs))
        if it == ITERS - 1:
            order = [lax.rem(z + j, zs) for j in range(1, zs + 1)]
        for j, g in enumerate(order):
            total = jnp.zeros((width, scenarios), F32)
            for k in range(slots):
                hit = jnp.logical_and(alive[k], rows_of[k] == g)
                total = total + jnp.where(hit, terms[k], 0.0)
            totals[g] = total
            outgoing[g] = total.astype(BF16)
            planes.append([])
            for e in range(1, ps):
                theirs = pl.ds(pl.multiple_of(lax.rem(p + e, ps) * own, own), own)
                planes[j].append(
                    remote(
                        outgoing.at[g, theirs, :],
                        plane_in.at[e - 1, g],
                        plane_send.at[it, j, e],
                        plane_recv.at[it, j, e],
                        p_peer(e),
                    )
                )
        if it == 0:
            for copy in fetched:
                copy.wait_recv()
            for g in range(zs):
                sigma[g] = spread(sigma_ref[g], scenarios)

        columns = []
        for j, g in enumerate(order):
            total = totals[g, mine, :]
            for e in range(1, ps):
                planes[j][e - 1].wait_recv()
                total = total + plane_in[e - 1, g].astype(F32)
            if it < ITERS - 1:
                column_sums[g] = total
                column_outs[g] = total.astype(BF16)
                part = column_outs.at[g]
                columns.append(
                    [
                        remote(
                            part,
                            column_ins.at[g, d - 1],
                            column_send.at[g, d],
                            column_recv.at[g, d],
                            z_peer(d),
                        )
                        for d in range(1, zs)
                    ]
                )
            elif j < zs - 1:
                last_outs[j] = total.astype(BF16)
                columns.append(
                    remote(
                        last_outs.at[j],
                        last_ins.at[j],
                        last_send.at[j],
                        last_recv.at[j],
                        z_peer(j + 1),
                    )
                )
            else:
                forward = total
    for j, copy in enumerate(columns):
        copy.wait_recv()
        forward = forward + last_ins[j].astype(F32)
    dual[z] = jnp.maximum(dual[z] + sigma[z] * (demand[...] - forward), 0.0)

    store = pltpu.make_async_copy(dual.at[z], dual_out.at[0], local_sem.at[1])
    store.start()
    stores.append(store)
    for copy in sent:
        copy.wait_send()
    for store in stores:
        store.wait()


def on_device(
    k_blocks,
    slot_row,
    slot_col,
    live_count,
    cost,
    upper,
    tau,
    sigma,
    demand,
    primal_start,
    dual_start,
):
    _, _, slots, width, _ = k_blocks.shape
    _, own, scenarios = dual_start.shape
    variables = primal_start.shape[0]
    col_blocks = variables // width
    rs = lax.axis_size("row")
    ps = width // own
    zs = lax.axis_size("col") // ps
    flat = lambda v: v.reshape(-1, 128)
    anywhere = pl.BlockSpec(memory_space=pl.ANY)
    dma = pltpu.SemaphoreType.DMA
    twice = lambda shape, kind: [pltpu.VMEM(shape, kind) for _ in range(ITERS)]
    return pl.pallas_call(
        functools.partial(kernel, (zs, ps, rs)),
        out_shape=(
            jax.ShapeDtypeStruct(primal_start.shape, F32),
            jax.ShapeDtypeStruct(dual_start.shape, F32),
        ),
        in_specs=[anywhere] * 11,
        out_specs=(anywhere, anywhere),
        scratch_shapes=[
            pltpu.SMEM((1, 1, slots), jnp.int32),
            pltpu.SMEM((1, 1, slots), jnp.int32),
            pltpu.SMEM((1, 1), jnp.int32),
            pltpu.VMEM((variables // 128, 128), F32),
            pltpu.VMEM((variables // 128, 128), F32),
            pltpu.VMEM((variables // 128, 128), F32),
            pltpu.VMEM((zs, 1, own), F32),
            pltpu.VMEM((slots, width, width), BF16),
            pltpu.VMEM((slots, width, width), BF16),
            pltpu.VMEM((variables, scenarios), F32),
            pltpu.VMEM((zs, own, scenarios), F32),
            pltpu.VMEM((own, scenarios), F32),
            pltpu.VMEM((variables, scenarios), F32),
            pltpu.VMEM((variables, scenarios), F32),
            pltpu.VMEM((variables, scenarios), F32),
            pltpu.VMEM((zs, own, scenarios), F32),
            pltpu.VMEM((slots, width, scenarios), F32),
            pltpu.VMEM((col_blocks, width, scenarios), BF16),
            twice((zs, width, scenarios), BF16),
            twice((rs, col_blocks, width, scenarios), F32),
            twice((zs, width, scenarios), BF16),
            pltpu.VMEM((zs, width, scenarios), F32),
            pltpu.VMEM((zs, own, scenarios), F32),
            pltpu.VMEM((zs, own, scenarios), F32),
            twice((ps - 1, zs, own, scenarios), BF16),
            pltpu.VMEM((zs, own, scenarios), BF16),
            pltpu.VMEM((zs, zs - 1, own, scenarios), BF16),
            pltpu.VMEM((zs - 1, own, scenarios), BF16),
            pltpu.VMEM((zs - 1, own, scenarios), BF16),
            dma((11,)),
            dma((ITERS, zs, ps)),
            dma((ITERS, zs, ps)),
            dma((ITERS, rs, col_blocks)),
            dma((ITERS, rs, col_blocks)),
            dma((ITERS, zs, ps)),
            dma((ITERS, zs, ps)),
            dma((zs, zs)),
            dma((zs, zs)),
            dma((4, zs)),
            dma((4, zs)),
            dma((zs,)),
            dma((zs,)),
        ],
        compiler_params=pltpu.CompilerParams(
            collective_id=0, has_side_effects=True, vmem_limit_bytes=60 * 1024 * 1024
        ),
        cost_estimate=pl.CostEstimate(
            flops=ITERS * 4 * slots * width * width * scenarios,
            bytes_accessed=2 * slots * width * width + 8 * variables * scenarios,
            transcendentals=0,
        ),
    )(
        slot_row,
        slot_col,
        live_count,
        k_blocks,
        flat(cost),
        flat(upper),
        flat(tau),
        sigma,
        demand,
        primal_start,
        dual_start,
    )


def solution(mesh):
    in_specs = (
        P("row", "col", None, None, None),
        P("row", "col", None),
        P("row", "col", None),
        P("row", "col"),
        P("col"),
        P("col"),
        P("col"),
        P("row", "col"),
        P("row", "col", None),
        P("col", None),
        P("row", "col", None),
    )
    out_specs = (P("col", None), P("row", "col", None))
    return jax.shard_map(
        on_device, mesh=mesh, in_specs=in_specs, out_specs=out_specs, check_vma=False
    )
```

time: 50.5 us -> 44.7 us (0.89)
  local copies, waits for them, and re-layouts: 7.04 us -> 2.49 us
  Pallas kernels: 41.7 us -> 40.8 us
    unnamed x22 -> x4, local copies, waits for them, and re-layouts: 7.04 us -> 2.49 us
    pallas_call x1, Pallas kernels: 41.7 us -> 40.8 us  [on_device(): pl.pallas_call(functools.partial(kernel, (zs, ps, rs)), out_shape=(jax.Sh...]
where the time goes in v2:
time: 44.7 us; the launch traced here: 44.6 us
  Pallas kernels  40.8 us (91%)
  local copies, waits for them, and re-layouts  2.49 us (6%)
  between operations  1.3 us (3%)
    pallas_call x1, Pallas kernels, on_device(): pl.pallas_call(functools.partial(kernel, (zs, ps, rs)), out_shape=(jax.Sh...  40.8 us
    unnamed x4, local copies, waits for them, and re-layouts  2.49 us

profile of v2, /device:TPU:0, one launch (start us, length us, event | category | flops | bytes accessed | tf_op | source)
XLA Modules:
  0.0 44.6 jit_solution(17334290197100009905)
XLA Ops:
  1.3 40.8 %shard_map.122 = (f32[1024,128]{1,0:T(8,128)}, f32[1,64,128]{2,1,0:T(8,128)}) custom-call(s32[1,1,4]{2,1,0:T(1,128)} %slot_row_hbm.1, s32[1,1,4]{2,1,0:T(1,128)} %slot_col_hbm.1, s32[1,1]{1,0:T(1,128)S(6)} %copy.15.live_count_hbm, bf16[1,1,4,256,256]{4,3,2,1,0:T(8,128)(2,1)} %k_hbm.1, f32[8,128]{1,0:T(8,128)} %bitcast.3, f32[8,128]{1,0:T(8,128)} %bitcast.4, ...), custom_call_target="tpu_custom_call" | custom-call | flops 268435456 | bytes 1572864 | tf_op jit(solution)/shard_map/pallas_call | solution.py:357
  42.1 0.0 copy-start
  42.1 1.9 %copy.16 = f32[1024,128]{1,0:T(8,128)} copy(f32[1024,128]{1,0:T(8,128)} %get-tuple-element.4) | data formatting | bytes 1048576
  44.0 0.0 copy-done
  44.0 0.6 %copy.17 = f32[1,64,128]{2,1,0:T(8,128)} copy(f32[1,64,128]{2,1,0:T(8,128)S(1)} %copy-done) | data formatting | bytes 65536
Async XLA Ops:
  42.1 1.9 %copy-start = (f32[1,64,128]{2,1,0:T(8,128)S(1)}, f32[1,64,128]{2,1,0:T(8,128)}, u32[]{:S(2)}) copy-start(f32[1,64,128]{2,1,0:T(8,128)} %get-tuple-element.5) | copy-start | bytes 98308

commit v3 on v2

--- a/solution.py
+++ b/solution.py
@@ -135,25 +135,6 @@
     loads[0].wait()
     everyones[0][z, mine, :] = dual[z].astype(BF16)
 
-    for load in loads[3:8]:
-        load.wait()
-    chunk = cost_ref.shape[1]
-    for i in range(cost_ref.shape[0]):
-        at = pl.ds(i * chunk, chunk)
-        cost[at, :] = spread(cost_ref[i : i + 1, :], scenarios)
-        upper[at, :] = spread(upper_ref[i : i + 1, :], scenarios)
-        tau[at, :] = spread(tau_ref[i : i + 1, :], scenarios)
-    loads[1].wait()
-    ahead[z] = dual[z] + spread(sigma_ref[z], scenarios) * demand[...]
-    for k in range(slots):
-        blocks_t[k] = blocks[k].T
-    for load in loads[8:]:
-        load.wait()
-    live = live_count[0, 0]
-    alive = [k < live for k in range(slots)]
-    rows_of = [slot_row[0, 0, k] for k in range(slots)]
-    cols_of = [slot_col[0, 0, k] for k in range(slots)]
-
     pl.semaphore_wait(barrier, len(peers))
 
     sent = []
@@ -191,9 +172,28 @@
                 for d in range(1, zs)
             ]
             in_plane += [pass_on(z, e) for e in range(1, ps)]
+            loads[1].wait()
+            for k in range(slots):
+                blocks_t[k] = blocks[k].T
             for d in range(1, zs):
                 along_z[d - 1].wait_recv()
                 in_plane += [pass_on(back_z(d), e) for e in range(1, ps)]
+            for load in loads[8:]:
+                load.wait()
+            live = live_count[0, 0]
+            alive = [k < live for k in range(slots)]
+            rows_of = [slot_row[0, 0, k] for k in range(slots)]
+            cols_of = [slot_col[0, 0, k] for k in range(slots)]
+
+            for load in loads[3:8]:
+                load.wait()
+            chunk = cost_ref.shape[1]
+            for i in range(cost_ref.shape[0]):
+                at = pl.ds(i * chunk, chunk)
+                cost[at, :] = spread(cost_ref[i : i + 1, :], scenarios)
+                upper[at, :] = spread(upper_ref[i : i + 1, :], scenarios)
+                tau[at, :] = spread(tau_ref[i : i + 1, :], scenarios)
+            ahead[z] = dual[z] + spread(sigma_ref[z], scenarios) * demand[...]
         else:
             for g in range(zs):
                 forward = column_sums[g]

time: 44.7 us -> 44.4 us (level)
  no operation moved by 1% of the time
where the time goes in v3:
time: 44.4 us; the launch traced here: 44.3 us
  Pallas kernels  40.5 us (91%)
  local copies, waits for them, and re-layouts  2.49 us (6%)
  between operations  1.3 us (3%)
    pallas_call x1, Pallas kernels, on_device(): pl.pallas_call(functools.partial(kernel, (zs, ps, rs)), out_shape=(jax.Sh...  40.5 us
    unnamed x4, local copies, waits for them, and re-layouts  2.49 us

profile of v3, /device:TPU:0, one launch (start us, length us, event | category | flops | bytes accessed | tf_op | source)
XLA Modules:
  0.0 44.3 jit_solution(13455828157053224332)
XLA Ops:
  1.3 40.5 %shard_map.122 = (f32[1024,128]{1,0:T(8,128)}, f32[1,64,128]{2,1,0:T(8,128)}) custom-call(s32[1,1,4]{2,1,0:T(1,128)} %slot_row_hbm.1, s32[1,1,4]{2,1,0:T(1,128)} %slot_col_hbm.1, s32[1,1]{1,0:T(1,128)S(6)} %copy.15.live_count_hbm, bf16[1,1,4,256,256]{4,3,2,1,0:T(8,128)(2,1)} %k_hbm.1, f32[8,128]{1,0:T(8,128)} %bitcast.3, f32[8,128]{1,0:T(8,128)} %bitcast.4, ...), custom_call_target="tpu_custom_call" | custom-call | flops 268435456 | bytes 1572864 | tf_op jit(solution)/shard_map/pallas_call | solution.py:357
  41.8 0.0 copy-start
  41.8 1.9 %copy.16 = f32[1024,128]{1,0:T(8,128)} copy(f32[1024,128]{1,0:T(8,128)} %get-tuple-element.4) | data formatting | bytes 1048576
  43.6 0.0 copy-done
  43.7 0.6 %copy.17 = f32[1,64,128]{2,1,0:T(8,128)} copy(f32[1,64,128]{2,1,0:T(8,128)S(1)} %copy-done) | data formatting | bytes 65536
Async XLA Ops:
  41.8 1.9 %copy-start = (f32[1,64,128]{2,1,0:T(8,128)S(1)}, f32[1,64,128]{2,1,0:T(8,128)}, u32[]{:S(2)}) copy-start(f32[1,64,128]{2,1,0:T(8,128)} %get-tuple-element.5) | copy-start | bytes 98308
